TPU v7x, 32 devices: a whole 2x2x4 slice. The times are simulated.
32 devices in a mesh: row: 8 (over z, core), col: 4 (over y, x).
Axes of the slice: x: 2, y: 2, z: 4, core: 2. Of those that a mesh axis runs over, the one named last changes fastest.
Arguments:
- cost_tiles: float32 [8, 4, 64, 128, 128], P('row', 'col'), may hold values from 0 to 66
- tile_rows: int32 [8, 4, 64], P('row', 'col'), may hold values from 0 to 127, as said below
- tile_cols: int32 [8, 4, 64], P('row', 'col'), may hold values from 0 to 127
- tile_count: int32 [8, 4], P('row', 'col'), may hold values from 32 to 64, as said below
- source_logmass: float32 [131072], P('row'), may hold values from -3 to 0
- target_logmass: float32 [65536], P('col'), may hold values from -103 to -100
- target_init: float32 [65536], P('col'), may hold values from -2 to 14
Outputs:
- source_potential: float32 [131072], P('row')
- target_potential: float32 [65536], P('col')
Inputs may be any that keep to these rules, and one draw needn't show every extreme that they name: Among the first tile_count slots of a device all (tile_rows, tile_cols) pairs differ; every source block of a row shard appears in such a slot of some device of that shard, and every target block of a col shard likewise. Slots at tile_count or later hold pairs to be ignored. `tile_count`: some device has all 64 slots in use in every draw.
All inputs are finite; a program needn't handle non-finite values.
Results may differ from a plain program's by a relative error of at most 0.00019.
Values sent between devices are 32-bit elements; how exact they have to be, the bound alone decides.
A program may use at most 64 MiB of HBM per device.

v0:
```python
import jax
import jax.numpy as jnp
from jax import lax
from jax.sharding import PartitionSpec as P

ITERS = 2


EPS = 0.1


def joined(shard, axis, combine):
    everything = jax.tree.map(lambda part: lax.all_gather(part, axis), shard)
    initial = jax.tree.map(lambda part: part[0], everything)

    def step(k, so_far):
        return combine(so_far, jax.tree.map(lambda part: part[k], everything))

    return lax.fori_loop(1, lax.axis_size(axis), step, initial)


def block_stats(cost, pot_blocks, gather_ids, seg_ids, valid, nseg, rows_side):
    red = 2 if rows_side else 1
    part = pot_blocks[gather_ids]
    if rows_side:
        scores = (part[:, None, :] - cost) / EPS
    else:
        scores = (part[:, :, None] - cost) / EPS
    tmax = jnp.where(valid[:, None], jnp.max(scores, axis=red), -jnp.inf)
    onehot = (seg_ids[:, None] == jnp.arange(nseg)[None, :]) & valid[:, None]
    peak = jnp.max(jnp.where(onehot.T[:, :, None], tmax[None, :, :], -jnp.inf), axis=1)
    shift = jnp.where(valid[:, None], peak[seg_ids], 0.0)
    if rows_side:
        expo = jnp.exp(scores - shift[:, :, None])
    else:
        expo = jnp.exp(scores - shift[:, None, :])
    tsum = jnp.where(valid[:, None], jnp.sum(expo, axis=red), 0.0)
    mass = jnp.dot(
        onehot.astype(jnp.float32).T,
        tsum,
        precision=lax.Precision.HIGHEST,
        preferred_element_type=jnp.float32,
    )
    return (peak, mass)


def pair_combine(first, second):
    top = jnp.maximum(first[0], second[0])
    safe = jnp.where(jnp.isfinite(top), top, 0.0)
    return (top, first[1] * jnp.exp(first[0] - safe) + second[1] * jnp.exp(second[0] - safe))


def local_stats(cost, pot, gather_ids, seg_ids, count, nseg, rows_side):
    pot_blocks = pot.reshape(-1, cost.shape[-1])
    slots = cost.shape[0]
    valid = jnp.arange(slots) < count
    return block_stats(cost, pot_blocks, gather_ids, seg_ids, valid, nseg, rows_side)


def finish_source(peak, mass, logmass):
    top, total = joined((peak, mass), "col", pair_combine)
    return EPS * logmass - EPS * (top + jnp.log(total)).reshape(-1)


def finish_target(peak, mass, logmass):
    top, total = joined((peak, mass), "row", pair_combine)
    return EPS * logmass - EPS * (top + jnp.log(total)).reshape(-1)


def local(
    cost_tiles, tile_rows, tile_cols, tile_count, source_logmass, target_logmass, target_init
):
    width = cost_tiles.shape[-1]
    cost = cost_tiles.reshape(cost_tiles.shape[2], width, width)
    rows = tile_rows.reshape(-1)
    cols = tile_cols.reshape(-1)
    count = tile_count.reshape(())
    src_blocks = source_logmass.shape[0] // width
    tgt_blocks = target_logmass.shape[0] // width
    target_potential = target_init
    source_potential = source_logmass
    for step in range(ITERS):
        peak, mass = local_stats(cost, target_potential, cols, rows, count, src_blocks, True)
        source_potential = finish_source(peak, mass, source_logmass)
        peak, mass = local_stats(cost, source_potential, rows, cols, count, tgt_blocks, False)
        target_potential = finish_target(peak, mass, target_logmass)
    return (source_potential, target_potential)


def solution(mesh):
    return jax.shard_map(
        local,
        mesh=mesh,
        in_specs=(
            P("row", "col", None, None, None),
            P("row", "col", None),
            P("row", "col", None),
            P("row", "col"),
            P("row"),
            P("col"),
            P("col"),
        ),
        out_specs=(P("row"), P("col")),
        check_vma=False,
    )
```

profile of v0, /device:TPU:0, one launch (start us, length us, event | category | flops | bytes accessed | tf_op | source)
XLA Modules:
  0.0 141.2 jit_solution(17372238942863826016)
XLA Ops:
  1.4 0.1 copy-done
  1.5 0.7 fusion.47
  2.1 0.7 fusion.46
  2.8 0.6 gather_fusion
  3.4 3.3 %fusion.15 = f32[64,128]{1,0:T(8,128)S(1)} fusion(f32[1,1,64,128,128]{4,3,2,1,0:T(8,128)} %param.15, f32[64,128]{1,0:T(8,128)S(1)} %gather_fusion), kind=kLoop, calls=%fused_computation.51 | loop fusion | flops 3137536 | bytes 4259840 | tf_op jit(solution)/shard_map/reduce_max | solution.py:29
  6.8 0.1 broadcast_select_fusion.7
  6.9 1.6 %select_reduce_fusion.3 = f32[128,128]{1,0:T(8,128)S(1)} fusion(f32[64,128]{1,0:T(8,128)S(1)} %broadcast_select_fusion.7, pred[128,64]{1,0:T(8,128)(4,1)S(1)} %get-tuple-element.591), kind=kLoop, calls=%fused_computation.47 | loop fusion | flops 2080768 | bytes 106496 | tf_op jit(solution)/shard_map/reduce_max | solution.py:31
  8.5 0.6 gather_fusion.1
  9.1 0.1 broadcast_select_fusion.3
  9.2 4.0 %exponential_reduce_fusion.3 = f32[64,128]{1,0:T(8,128)S(1)} fusion(f32[1,1,64,128,128]{4,3,2,1,0:T(8,128)} %param.15, f32[64,128]{1,0:T(8,128)S(1)} %broadcast_select_fusion.3, f32[64,128]{1,0:T(8,128)S(1)} %gather_fusion), kind=kLoop, calls=%fused_computation.46 | loop fusion | flops 4186112 | bytes 4292608 | tf_op jit(solution)/shard_map/reduce_sum | solution.py:37
  13.2 0.3 fusion.26
  13.5 10.4 %all-gather.1 = f32[512,128]{1,0:T(8,128)S(1)} all-gather(f32[128,128]{1,0:T(8,128)S(1)} %fusion.26), channel_id=3, replica_groups=mesh['row'=8,'col'=4] {'col'}, dimensions={0}, use_global_device_ids=true | all-gather | bytes 327680 | tf_op jit(solution)/shard_map/all_gather | solution.py:13
  23.9 9.0 %all-gather = f32[512,128]{1,0:T(8,128)S(1)} all-gather(f32[128,128]{1,0:T(8,128)S(1)} %select_reduce_fusion.3), channel_id=2, replica_groups=mesh['row'=8,'col'=4] {'col'}, dimensions={0}, use_global_device_ids=true | all-gather | bytes 327680 | tf_op jit(solution)/shard_map/all_gather | solution.py:13
  32.9 0.2 while.68
  33.2 0.6 gather_fusion.2
  33.8 2.8 %fusion.14 = f32[64,128]{1,0:T(8,128)S(1)} fusion(f32[1,1,64,128,128]{4,3,2,1,0:T(8,128)} %param.15, f32[64,128]{1,0:T(8,128)S(1)} %gather_fusion.2), kind=kLoop, calls=%fused_computation.50 | loop fusion | flops 3137536 | bytes 4259840 | tf_op jit(solution)/shard_map/reduce_max | solution.py:29
  36.7 0.1 broadcast_select_fusion.6
  36.7 1.6 %select_reduce_fusion.2 = f32[128,128]{1,0:T(8,128)S(1)} fusion(f32[64,128]{1,0:T(8,128)S(1)} %broadcast_select_fusion.6, pred[128,64]{1,0:T(8,128)(4,1)S(1)} %get-tuple-element.590), kind=kLoop, calls=%fused_computation.45 | loop fusion | flops 2080768 | bytes 106496 | tf_op jit(solution)/shard_map/reduce_max | solution.py:31
  38.4 0.6 gather_fusion.3
  39.0 0.1 broadcast_select_fusion.2
  39.0 2.9 %exponential_reduce_fusion.2 = f32[64,128]{1,0:T(8,128)S(1)} fusion(f32[1,1,64,128,128]{4,3,2,1,0:T(8,128)} %param.15, f32[64,128]{1,0:T(8,128)S(1)} %broadcast_select_fusion.2, f32[64,128]{1,0:T(8,128)S(1)} %gather_fusion.2), kind=kLoop, calls=%fused_computation.44 | loop fusion | flops 4186112 | bytes 4292608 | tf_op jit(solution)/shard_map/reduce_sum | solution.py:37
  42.0 0.3 fusion.24
  42.3 15.4 %all-gather.3 = f32[1024,128]{1,0:T(8,128)S(1)} all-gather(f32[128,128]{1,0:T(8,128)S(1)} %fusion.24), channel_id=5, replica_groups=mesh['row'=8,'col'=4] {'row'}, dimensions={0}, use_global_device_ids=true | all-gather | bytes 589824 | tf_op jit(solution)/shard_map/all_gather | solution.py:13
  57.7 14.7 %all-gather.2 = f32[1024,128]{1,0:T(8,128)S(1)} all-gather(f32[128,128]{1,0:T(8,128)S(1)} %select_reduce_fusion.2), channel_id=4, replica_groups=mesh['row'=8,'col'=4] {'row'}, dimensions={0}, use_global_device_ids=true | all-gather | bytes 589824 | tf_op jit(solution)/shard_map/all_gather | solution.py:13
  72.4 0.5 while.69
  73.0 0.6 gather_fusion.4
  73.6 3.3 %fusion.13 = f32[64,128]{1,0:T(8,128)S(1)} fusion(f32[1,1,64,128,128]{4,3,2,1,0:T(8,128)} %param.15, f32[64,128]{1,0:T(8,128)S(1)} %gather_fusion.4), kind=kLoop, calls=%fused_computation.49 | loop fusion | flops 3137536 | bytes 4259840 | tf_op jit(solution)/shard_map/reduce_max | solution.py:29
  76.9 0.1 broadcast_select_fusion.5
  77.0 1.6 %select_reduce_fusion.1 = f32[128,128]{1,0:T(8,128)S(1)} fusion(f32[64,128]{1,0:T(8,128)S(1)} %broadcast_select_fusion.5, pred[128,64]{1,0:T(8,128)(4,1)S(1)} %get-tuple-element.591), kind=kLoop, calls=%fused_computation.43 | loop fusion | flops 2080768 | bytes 106496 | tf_op jit(solution)/shard_map/reduce_max | solution.py:31
  78.6 0.6 gather_fusion.5
  79.2 0.1 broadcast_select_fusion.1
  79.3 4.0 %exponential_reduce_fusion.1 = f32[64,128]{1,0:T(8,128)S(1)} fusion(f32[1,1,64,128,128]{4,3,2,1,0:T(8,128)} %param.15, f32[64,128]{1,0:T(8,128)S(1)} %broadcast_select_fusion.1, f32[64,128]{1,0:T(8,128)S(1)} %gather_fusion.4), kind=kLoop, calls=%fused_computation.42 | loop fusion | flops 4186112 | bytes 4292608 | tf_op jit(solution)/shard_map/reduce_sum | solution.py:37
  83.3 0.3 fusion.22
  83.6 8.1 %all-gather.5 = f32[512,128]{1,0:T(8,128)S(1)} all-gather(f32[128,128]{1,0:T(8,128)S(1)} %fusion.22), channel_id=7, replica_groups=mesh['row'=8,'col'=4] {'col'}, dimensions={0}, use_global_device_ids=true | all-gather | bytes 327680 | tf_op jit(solution)/shard_map/all_gather | solution.py:13
  91.7 9.1 %all-gather.4 = f32[512,128]{1,0:T(8,128)S(1)} all-gather(f32[128,128]{1,0:T(8,128)S(1)} %select_reduce_fusion.1), channel_id=6, replica_groups=mesh['row'=8,'col'=4] {'col'}, dimensions={0}, use_global_device_ids=true | all-gather | bytes 327680 | tf_op jit(solution)/shard_map/all_gather | solution.py:13
  100.8 0.2 while.70
  101.1 0.6 gather_fusion.6
  101.7 2.8 %fusion.12 = f32[64,128]{1,0:T(8,128)S(1)} fusion(f32[1,1,64,128,128]{4,3,2,1,0:T(8,128)} %param.15, f32[64,128]{1,0:T(8,128)S(1)} %gather_fusion.6), kind=kLoop, calls=%fused_computation.48 | loop fusion | flops 3137536 | bytes 4259840 | tf_op jit(solution)/shard_map/reduce_max | solution.py:29
  104.5 0.1 broadcast_select_fusion.4
  104.6 1.6 %select_reduce_fusion = f32[128,128]{1,0:T(8,128)S(1)} fusion(f32[64,128]{1,0:T(8,128)S(1)} %broadcast_select_fusion.4, pred[128,64]{1,0:T(8,128)(4,1)S(1)} %get-tuple-element.590), kind=kLoop, calls=%fused_computation.41 | loop fusion | flops 2080768 | bytes 106496 | tf_op jit(solution)/shard_map/reduce_max | solution.py:31
  106.2 0.6 gather_fusion.7
  106.8 0.1 broadcast_select_fusion
  106.9 2.9 %exponential_reduce_fusion = f32[64,128]{1,0:T(8,128)S(1)} fusion(f32[1,1,64,128,128]{4,3,2,1,0:T(8,128)} %param.15, f32[64,128]{1,0:T(8,128)S(1)} %broadcast_select_fusion, f32[64,128]{1,0:T(8,128)S(1)} %gather_fusion.6), kind=kLoop, calls=%fused_computation.40 | loop fusion | flops 4186112 | bytes 4292608 | tf_op jit(solution)/shard_map/reduce_sum | solution.py:37
  109.8 0.3 fusion.20
  110.1 15.1 %all-gather.7 = f32[1024,128]{1,0:T(8,128)S(1)} all-gather(f32[128,128]{1,0:T(8,128)S(1)} %fusion.20), channel_id=9, replica_groups=mesh['row'=8,'col'=4] {'row'}, dimensions={0}, use_global_device_ids=true | all-gather | bytes 589824 | tf_op jit(solution)/shard_map/all_gather | solution.py:13
  125.3 14.7 %all-gather.6 = f32[1024,128]{1,0:T(8,128)S(1)} all-gather(f32[128,128]{1,0:T(8,128)S(1)} %select_reduce_fusion), channel_id=8, replica_groups=mesh['row'=8,'col'=4] {'row'}, dimensions={0}, use_global_device_ids=true | all-gather | bytes 589824 | tf_op jit(solution)/shard_map/all_gather | solution.py:13
  140.0 0.5 while.71
  140.5 0.7 bitcast_subtract_fusion.8
  (46 shorter events, 1.3 us)
Async XLA Ops:
  0.6 0.8 copy-start
  0.6 6.2 %copy-start.5 = (s32[1,1,64]{2,1,0:T(1,128)S(1)}, s32[1,1,64]{2,1,0:T(1,128)}, u32[]{:S(2)}) copy-start(s32[1,1,64]{2,1,0:T(1,128)} %param.17) | copy-start | bytes 772
  0.7 6.2 %copy-start.4 = (s32[1,1,64]{2,1,0:T(1,128)S(1)}, s32[1,1,64]{2,1,0:T(1,128)}, u32[]{:S(2)}) copy-start(s32[1,1,64]{2,1,0:T(1,128)} %param.16) | copy-start | bytes 772
  6.8 26.4 %copy-start.2 = (f32[16384]{0:T(1024)S(1)}, f32[16384]{0:T(1024)}, u32[]{:S(2)}) copy-start(f32[16384]{0:T(1024)} %param.19) | copy-start | bytes 196612
  38.4 34.6 %copy-start.3 = (f32[16384]{0:T(1024)S(1)}, f32[16384]{0:T(1024)}, u32[]{:S(2)}) copy-start(f32[16384]{0:T(1024)} %param.20) | copy-start | bytes 196612
  101.1 8.7 %copy-start.1 = (f32[16384]{0:T(1024)}, f32[16384]{0:T(1024)S(1)}, u32[]{:S(2)}) copy-start(f32[16384]{0:T(1024)S(1)} %bitcast_subtract_fusion.9) | copy-start | bytes 196612
where the time goes:
time: 142 us; the launch traced here: 141 us
  blocking collectives  96.6 us (68%)
  other arithmetic  36.3 us (26%)
  local copies, waits for them, and re-layouts  4.97 us (4%)
  between operations  1.6 us (1%)
    all_gather x8, blocking collectives, joined(): everything = jax.tree.map(lambda part: lax.all_gather(part, axis), shard)  96.6 us
    reduce_sum x4, other arithmetic, block_stats(): tsum = jnp.where(valid[:, None], jnp.sum(expo, axis=red), 0.0)  13.8 us
    reduce_max x4, other arithmetic, block_stats(): tmax = jnp.where(valid[:, None], jnp.max(scores, axis=red), -jnp.inf)  12.4 us
    reduce_max x4, other arithmetic, block_stats(): jnp.max(jnp.where(onehot.T[:, :, None], tmax[None, :, :], -jnp.inf), axis=1)  6.41 us

commit v1 on v0

v1 whole, which is shorter than its diff:
```python
import functools
import math

import jax
import jax.numpy as jnp
from jax import lax
from jax.experimental import pallas as pl
from jax.experimental.pallas import tpu as pltpu
from jax.sharding import PartitionSpec as P

ITERS = 2
EPS = 0.1
LOG2E = math.log2(math.e)
SCALE = LOG2E / EPS
GROUP = 8
LANES = 128
MESH = pl.DeviceIdType.MESH


def split_bf16(x, parts):
    out = []
    for _ in range(parts):
        head = x.astype(jnp.bfloat16)
        out.append(head)
        x = x - head.astype(jnp.float32)
    return out


def kernel(
    cost, rows, cols, count, slog, tlog, tinit,
    s_out, t_out,
    cbuf, lbuf, gbuf, init_pot, seg_s, seg_t, hot_s, hot_t, rep_s, rep_t,
    part_s0, part_s1, part_t0, part_t1,
    mid_s0, mid_s1, mid_t0, mid_t1,
    pot_s0, pot_s1, pot_t0, pot_t1,
    cost_sem, scatter_send_s, scatter_recv_s, gather_send_s, gather_recv_s,
    scatter_send_t, scatter_recv_t, gather_send_t, gather_recv_t,
    *, n_row, n_col,
):
    cap = cbuf.shape[0]
    me = {"row": lax.axis_index("row"), "col": lax.axis_index("col")}
    sizes = {"row": n_row, "col": n_col}

    def peer(axis, o):
        return lax.rem(me[axis] + o, sizes[axis])

    barrier = pltpu.get_barrier_semaphore()
    for axis in ("col", "row"):
        for o in range(1, sizes[axis]):
            pl.semaphore_signal(
                barrier, inc=1, device_id={axis: peer(axis, o)}, device_id_type=MESH
            )

    groups = cap // GROUP

    def fetch(g):
        span = pl.ds(g * GROUP, GROUP)
        return pltpu.make_async_copy(cost.at[0, 0, span], cbuf.at[span], cost_sem.at[g])

    for g in range(groups):
        fetch(g).start()

    total = count[0, 0]
    lane = lax.broadcasted_iota(jnp.int32, (LANES, LANES), 1)
    sub8 = lax.broadcasted_iota(jnp.int32, (GROUP, LANES), 0)
    slot = lax.broadcasted_iota(jnp.int32, (cap, LANES), 0)

    def segment(ids, s):
        return jnp.where(s < total, ids[0, 0, s], -1)

    def prepare(ids, seg, hot, rep):
        nb = hot.shape[0]

        def fill(g, _):
            value = jnp.zeros((GROUP, LANES), jnp.int32)
            for k in range(GROUP):
                value = jnp.where(sub8 == k, segment(ids, g * GROUP + k), value)
            seg[pl.ds(pl.multiple_of(g * GROUP, GROUP), GROUP), :] = value
            return 0

        lax.fori_loop(0, groups, fill, 0)
        mine = seg[...]

        def earlier(g, dup):
            for k in range(GROUP):
                t = g * GROUP + k
                same = (mine == segment(ids, t)) & (slot > t)
                dup = jnp.where(same, 1.0, dup)
            return dup

        dup = lax.fori_loop(0, groups, earlier, jnp.zeros((cap, LANES), jnp.float32))
        blocks = lax.broadcasted_iota(jnp.int32, (cap, nb), 1)
        one = jnp.where(mine[:, :nb] == blocks, 1.0, 0.0)
        first = one * (1.0 - dup[:, :nb])
        both = jnp.concatenate([one, first], axis=0).T
        one, first = both[:, :cap], both[:, cap:]
        hot[...] = jnp.concatenate([one, one], axis=1).astype(jnp.bfloat16)
        rep[...] = jnp.concatenate([first] * 4, axis=1).astype(jnp.bfloat16)

    init_pot[...] = tinit[...] * SCALE
    prepare(rows, seg_s, hot_s, rep_s)
    prepare(cols, seg_t, hot_t, rep_t)

    def row_pass(pot, first):
        def group(g, acc):
            base = g * GROUP
            if first:
                fetch(g).wait()
            for k in range(GROUP):
                s = base + k
                tile = cbuf[s]
                if first:
                    tile = tile * SCALE
                    cbuf[s] = tile
                x = pot[pl.ds(cols[0, 0, s], 1), :] - tile
                m = jnp.max(x, axis=1, keepdims=True)
                t = jnp.sum(jnp.exp2(x - m), axis=1, keepdims=True)
                acc = jnp.where(lane == s, m + jnp.log2(t), acc)
            return acc

        acc = lax.fori_loop(0, groups, group, jnp.zeros((LANES, LANES), jnp.float32))
        lbuf[...] = acc.T[:cap]

    def col_pass(pot):
        def collect(g, _):
            for k in range(GROUP):
                s = g * GROUP + k
                gbuf[pl.ds(s, 1), :] = pot[pl.ds(rows[0, 0, s], 1), :]
            return 0

        lax.fori_loop(0, groups, collect, 0)
        turned = gbuf[...].T

        def group(g, _):
            base = g * GROUP
            near = pltpu.roll(turned, lax.rem(LANES - base, LANES), 1)
            top = jnp.zeros((GROUP, LANES), jnp.float32)
            mass = jnp.ones((GROUP, LANES), jnp.float32)
            for k in range(GROUP):
                x = near[:, k : k + 1] - cbuf[base + k]
                m = jnp.max(x, axis=0, keepdims=True)
                t = jnp.sum(jnp.exp2(x - m), axis=0, keepdims=True)
                top = jnp.where(sub8 == k, m, top)
                mass = jnp.where(sub8 == k, t, mass)
            lbuf[pl.ds(pl.multiple_of(base, GROUP), GROUP), :] = top + jnp.log2(mass)
            return 0

        lax.fori_loop(0, groups, group, 0)

    def merge(ids, seg, hot, rep, part):
        mine = seg[...]
        own = lbuf[...]

        def widen(g, best):
            for k in range(GROUP):
                t = g * GROUP + k
                other = jnp.maximum(best, lbuf[pl.ds(t, 1), :])
                best = jnp.where(mine == segment(ids, t), other, best)
            return best

        best = lax.fori_loop(0, groups, widen, own)
        weight = jnp.concatenate(split_bf16(jnp.exp2(own - best), 2), axis=0)
        tops = split_bf16(best, 3)
        tops = jnp.concatenate(tops + [jnp.zeros_like(tops[0])], axis=0)
        mass = jnp.dot(hot[...], weight, preferred_element_type=jnp.float32)
        peak = jnp.dot(rep[...], tops, preferred_element_type=jnp.float32)
        part[...] = jnp.where(mass > 0.0, peak + jnp.log2(mass), -1e30)

    pending = []

    def exchange(axis, it, part, mid, pot, logmass, s_send, s_recv, g_send, g_recv):
        n = sizes[axis]
        chunk = part.shape[0] // n
        copies = []
        for o in range(1, n):
            to = peer(axis, o)
            copies.append(pltpu.make_async_remote_copy(
                src_ref=part.at[pl.ds(to * chunk, chunk)],
                dst_ref=mid.at[o - 1],
                send_sem=s_send.at[it, o - 1],
                recv_sem=s_recv.at[it, o - 1],
                device_id={axis: to},
                device_id_type=MESH,
            ))
            copies[-1].start()
        own = pl.ds(pl.multiple_of(me[axis] * chunk, chunk), chunk)
        parts = [part[own, :]]
        mass = logmass[own, :] * LOG2E
        for copy in copies:
            copy.wait_recv()
        parts += [mid[o] for o in range(n - 1)]
        top = functools.reduce(jnp.maximum, parts)
        total = functools.reduce(jnp.add, [jnp.exp2(p - top) for p in parts])
        pot[own, :] = mass - (top + jnp.log2(total))
        pending.extend(copies)
        copies = []
        for o in range(1, n):
            copies.append(pltpu.make_async_remote_copy(
                src_ref=pot.at[own],
                dst_ref=pot.at[own],
                send_sem=g_send.at[it, o - 1],
                recv_sem=g_recv.at[it, o - 1],
                device_id={axis: peer(axis, o)},
                device_id_type=MESH,
            ))
            copies[-1].start()
        for copy in copies:
            copy.wait_recv()
        pending.extend(copies)

    source = ((part_s0, mid_s0, pot_s0), (part_s1, mid_s1, pot_s1))
    target = ((part_t0, mid_t0, pot_t0), (part_t1, mid_t1, pot_t1))
    pot = init_pot
    for it in range(ITERS):
        part, mid, pot_s = source[it]
        row_pass(pot, it == 0)
        merge(rows, seg_s, hot_s, rep_s, part)
        if it == 0:
            pl.semaphore_wait(barrier, n_row + n_col - 2)
        exchange("col", it, part, mid, pot_s, slog,
                 scatter_send_s, scatter_recv_s, gather_send_s, gather_recv_s)
        part, mid, pot = target[it]
        col_pass(pot_s)
        merge(cols, seg_t, hot_t, rep_t, part)
        exchange("row", it, part, mid, pot, tlog,
                 scatter_send_t, scatter_recv_t, gather_send_t, gather_recv_t)
    s_out[...] = pot_s[...]
    t_out[...] = pot[...]
    for copy in pending:
        copy.wait_send()


def local(
    n_row, n_col,
    cost_tiles, tile_rows, tile_cols, tile_count, source_logmass, target_logmass, target_init,
):
    cap, width = cost_tiles.shape[2], cost_tiles.shape[-1]
    nbs = source_logmass.shape[0] // width
    nbt = target_logmass.shape[0] // width
    f32, bf16 = jnp.float32, jnp.bfloat16
    vmem = pl.BlockSpec(memory_space=pltpu.VMEM)
    smem = pl.BlockSpec(memory_space=pltpu.SMEM)
    dma = pltpu.SemaphoreType.DMA
    scratch = [
        pltpu.VMEM((cap, width, width), f32),
        pltpu.VMEM((cap, width), f32),
        pltpu.VMEM((cap, width), f32),
        pltpu.VMEM((nbt, width), f32),
        pltpu.VMEM((cap, width), jnp.int32),
        pltpu.VMEM((cap, width), jnp.int32),
        pltpu.VMEM((nbs, 2 * cap), bf16),
        pltpu.VMEM((nbt, 2 * cap), bf16),
        pltpu.VMEM((nbs, 4 * cap), bf16),
        pltpu.VMEM((nbt, 4 * cap), bf16),
    ]
    scratch += [pltpu.VMEM((nbs, width), f32)] * 2 + [pltpu.VMEM((nbt, width), f32)] * 2
    scratch += [pltpu.VMEM((n_col - 1, nbs // n_col, width), f32)] * 2
    scratch += [pltpu.VMEM((n_row - 1, nbt // n_row, width), f32)] * 2
    scratch += [pltpu.VMEM((nbs, width), f32)] * 2 + [pltpu.VMEM((nbt, width), f32)] * 2
    scratch += [dma((cap // GROUP,))]
    scratch += [dma((ITERS, n_col - 1))] * 4 + [dma((ITERS, n_row - 1))] * 4
    source, target = pl.pallas_call(
        functools.partial(kernel, n_row=n_row, n_col=n_col),
        out_shape=(
            jax.ShapeDtypeStruct((nbs, width), f32),
            jax.ShapeDtypeStruct((nbt, width), f32),
        ),
        in_specs=[pl.BlockSpec(memory_space=pl.ANY), smem, smem, smem, vmem, vmem, vmem],
        out_specs=(vmem, vmem),
        scratch_shapes=scratch,
        compiler_params=pltpu.CompilerParams(
            collective_id=0, has_side_effects=True, vmem_limit_bytes=48 * 1024 * 1024
        ),
        cost_estimate=pl.CostEstimate(
            flops=2 * ITERS * 5 * cap * width * width,
            bytes_accessed=4 * cap * width * width,
            transcendentals=2 * ITERS * cap * width * width,
        ),
    )(
        cost_tiles, tile_rows, tile_cols, tile_count,
        source_logmass.reshape(nbs, width),
        target_logmass.reshape(nbt, width),
        target_init.reshape(nbt, width),
    )
    return source.reshape(-1) / SCALE, target.reshape(-1) / SCALE


def solution(mesh):
    return jax.shard_map(
        functools.partial(local, mesh.shape["row"], mesh.shape["col"]),
        mesh=mesh,
        in_specs=(
            P("row", "col", None, None, None),
            P("row", "col", None),
            P("row", "col", None),
            P("row", "col"),
            P("row"),
            P("col"),
            P("col"),
        ),
        out_specs=(P("row"), P("col")),
        check_vma=False,
    )
```

time: 142 us -> 59.9 us (0.42)
  blocking collectives: 96.6 us -> 0 us
  Pallas kernels: 0 us -> 51.6 us
  other arithmetic: 36.3 us -> 0.66 us
    all_gather x8 -> x0, blocking collectives: 96.6 us -> none  [joined(): everything = jax.tree.map(lambda part: lax.all_gather(part, axis), shard)]
    pallas_call x0 -> x1, Pallas kernels: none -> 51.6 us  [local(): pl.pallas_call(functools.partial(kernel, n_row=n_row, n_col=n_col), out_s...]
    reduce_max x8 -> x0, other arithmetic: 18.8 us -> none  [the longest x4 12.4 us: block_stats(): tmax = jnp.where(valid[:, None], jnp.max(scores, axis=red), -jnp.inf)]
    reduce_sum x4 -> x0, other arithmetic: 13.8 us -> none  [block_stats(): tsum = jnp.where(valid[:, None], jnp.sum(expo, axis=red), 0.0)]
    unnamed x12, local copies, waits for them, and re-layouts: 0.15 us -> 6.01 us
    gather x8 -> x0, local copies, waits for them, and re-layouts: 4.78 us -> none  [the longest x4 2.39 us: block_stats(): shift = jnp.where(valid[:, None], peak[seg_ids], 0.0)]
    select_n x10 -> x0, other arithmetic: 1.91 us -> none  [the longest x5 0.96 us: block_stats(): shift = jnp.where(valid[:, None], peak[seg_ids], 0.0)]
where the time goes in v1:
time: 59.9 us; the launch traced here: 59.6 us
  Pallas kernels  51.6 us (86%)
  local copies, waits for them, and re-layouts  6.01 us (10%)
  between operations  1.3 us (2%)
  other arithmetic  0.66 us (1%)
    pallas_call x1, Pallas kernels, local(): pl.pallas_call(functools.partial(kernel, n_row=n_row, n_col=n_col), out_s...  51.6 us
    unnamed x12, local copies, waits for them, and re-layouts  6.01 us

profile of v1, /device:TPU:0, one launch (start us, length us, event | category | flops | bytes accessed | tf_op | source)
XLA Modules:
  0.0 59.6 jit_solution(3697814450085336690)
XLA Ops:
  1.3 0.0 copy-start
  1.3 2.2 %copy-done = f32[1,1,64,128,128]{4,3,2,1,0:T(8,128)S(1)} copy-done((f32[1,1,64,128,128]{4,3,2,1,0:T(8,128)S(1)}, f32[1,1,64,128,128]{4,3,2,1,0:T(8,128)}, u32[]{:S(2)}) %copy-start) | copy-done | bytes 4194328
  3.5 0.0 copy-start.1
  3.5 0.8 %copy-done.1 = f32[16384]{0:T(1024)S(1)} copy-done((f32[16384]{0:T(1024)S(1)}, f32[16384]{0:T(1024)}, u32[]{:S(2)}) %copy-start.1) | copy-done | bytes 65560
  4.3 0.0 copy-start.2
  4.3 0.8 %copy-done.2 = f32[16384]{0:T(1024)S(1)} copy-done((f32[16384]{0:T(1024)S(1)}, f32[16384]{0:T(1024)}, u32[]{:S(2)}) %copy-start.2) | copy-done | bytes 65560
  5.1 0.0 copy-start.3
  5.1 0.8 %copy-done.3 = f32[16384]{0:T(1024)S(1)} copy-done((f32[16384]{0:T(1024)S(1)}, f32[16384]{0:T(1024)}, u32[]{:S(2)}) %copy-start.3) | copy-done | bytes 65560
  6.0 0.0 copy-start.4
  6.0 0.7 %copy-done.4 = s32[1,1,64]{2,1,0:T(1,128)S(1)} copy-done((s32[1,1,64]{2,1,0:T(1,128)S(1)}, s32[1,1,64]{2,1,0:T(1,128)}, u32[]{:S(2)}) %copy-start.4) | copy-done | bytes 280
  6.6 0.0 copy-start.5
  6.6 0.7 %copy-done.5 = s32[1,1,64]{2,1,0:T(1,128)S(1)} copy-done((s32[1,1,64]{2,1,0:T(1,128)S(1)}, s32[1,1,64]{2,1,0:T(1,128)}, u32[]{:S(2)}) %copy-start.5) | copy-done | bytes 280
  7.3 51.6 %shard_map.86 = (f32[128,128]{1,0:T(8,128)S(1)}, f32[128,128]{1,0:T(8,128)S(1)}) custom-call(f32[1,1,64,128,128]{4,3,2,1,0:T(8,128)S(1)} %copy-done, s32[1,1,64]{2,1,0:T(1,128)S(1)} %copy-done.4, s32[1,1,64]{2,1,0:T(1,128)S(1)} %copy-done.5, s32[1,1]{1,0:T(1,128)S(6)} %copy.9.count, f32[128,128]{1,0:T(8,128)S(1)} %bitcast.7, f32[128,128]{1,0:T(8,128)S(1)} %bitcast.8, ...), custom_call_target="tpu_custom_call" | custom-call | flops 20971520 | bytes 4194304 | tf_op jit(solution)/shard_map/pallas_call | solution.py:262
  58.9 0.7 %multiply_bitcast_fusion = (f32[16384]{0:T(1024)}, f32[16384]{0:T(1024)}) fusion(f32[128,128]{1,0:T(8,128)S(1)} %get-tuple-element.5, f32[128,128]{1,0:T(8,128)S(1)} %get-tuple-element.4), kind=kLoop, calls=%fused_computation | loop fusion | flops 32768 | bytes 262144 | tf_op jit(solution)/shard_map/div | solution.py:285
Async XLA Ops:
  1.3 2.2 %copy-start = (f32[1,1,64,128,128]{4,3,2,1,0:T(8,128)S(1)}, f32[1,1,64,128,128]{4,3,2,1,0:T(8,128)}, u32[]{:S(2)}) copy-start(f32[1,1,64,128,128]{4,3,2,1,0:T(8,128)} %cost.1) | copy-start | bytes 12582916
  3.5 0.8 %copy-start.1 = (f32[16384]{0:T(1024)S(1)}, f32[16384]{0:T(1024)}, u32[]{:S(2)}) copy-start(f32[16384]{0:T(1024)} %param.11) | copy-start | bytes 196612
  4.3 0.8 %copy-start.2 = (f32[16384]{0:T(1024)S(1)}, f32[16384]{0:T(1024)}, u32[]{:S(2)}) copy-start(f32[16384]{0:T(1024)} %param.12) | copy-start | bytes 196612
  5.1 0.8 %copy-start.3 = (f32[16384]{0:T(1024)S(1)}, f32[16384]{0:T(1024)}, u32[]{:S(2)}) copy-start(f32[16384]{0:T(1024)} %param.13) | copy-start | bytes 196612
  6.0 0.7 %copy-start.4 = (s32[1,1,64]{2,1,0:T(1,128)S(1)}, s32[1,1,64]{2,1,0:T(1,128)}, u32[]{:S(2)}) copy-start(s32[1,1,64]{2,1,0:T(1,128)} %rows.1) | copy-start | bytes 772
  6.6 0.7 %copy-start.5 = (s32[1,1,64]{2,1,0:T(1,128)S(1)}, s32[1,1,64]{2,1,0:T(1,128)}, u32[]{:S(2)}) copy-start(s32[1,1,64]{2,1,0:T(1,128)} %cols.1) | copy-start | bytes 772

commit v2 on v1

--- a/solution.py
+++ b/solution.py
@@ -17,6 +17,12 @@
 MESH = pl.DeviceIdType.MESH
 
 
+def join(parts):
+    top = functools.reduce(jnp.maximum, parts)
+    total = functools.reduce(jnp.add, [jnp.exp2(p - top) for p in parts])
+    return top + jnp.log2(total)
+
+
 def split_bf16(x, parts):
     out = []
     for _ in range(parts):
@@ -27,9 +33,10 @@
 
 
 def kernel(
-    cost, rows, cols, count, slog, tlog, tinit,
+    cost, rows_in, cols_in, count, slog_in, tlog_in, tinit_in,
     s_out, t_out,
-    cbuf, lbuf, gbuf, init_pot, seg_s, seg_t, hot_s, hot_t, rep_s, rep_t,
+    rows, cols, slog, tlog, small_sem,
+    cbuf, turned_cost, fine, lbuf, gbuf, init_pot, seg_s, seg_t, hot_s, hot_t, rep_s, rep_t,
     part_s0, part_s1, part_t0, part_t1,
     mid_s0, mid_s1, mid_t0, mid_t1,
     pot_s0, pot_s1, pot_t0, pot_t1,
@@ -57,6 +64,14 @@
         span = pl.ds(g * GROUP, GROUP)
         return pltpu.make_async_copy(cost.at[0, 0, span], cbuf.at[span], cost_sem.at[g])
 
+    small = [
+        pltpu.make_async_copy(src, dst, small_sem.at[k])
+        for k, (src, dst) in enumerate((
+            (rows_in, rows), (cols_in, cols), (tinit_in, init_pot), (slog_in, slog), (tlog_in, tlog),
+        ))
+    ]
+    for copy in small:
+        copy.start()
     for g in range(groups):
         fetch(g).start()
 
@@ -97,35 +112,18 @@
         hot[...] = jnp.concatenate([one, one], axis=1).astype(jnp.bfloat16)
         rep[...] = jnp.concatenate([first] * 4, axis=1).astype(jnp.bfloat16)
 
-    init_pot[...] = tinit[...] * SCALE
+    gbuf[...] = jnp.zeros_like(gbuf)
+    for copy in small:
+        copy.wait()
+    init_pot[...] = init_pot[...] * SCALE
     prepare(rows, seg_s, hot_s, rep_s)
     prepare(cols, seg_t, hot_t, rep_t)
 
-    def row_pass(pot, first):
-        def group(g, acc):
-            base = g * GROUP
-            if first:
-                fetch(g).wait()
-            for k in range(GROUP):
-                s = base + k
-                tile = cbuf[s]
-                if first:
-                    tile = tile * SCALE
-                    cbuf[s] = tile
-                x = pot[pl.ds(cols[0, 0, s], 1), :] - tile
-                m = jnp.max(x, axis=1, keepdims=True)
-                t = jnp.sum(jnp.exp2(x - m), axis=1, keepdims=True)
-                acc = jnp.where(lane == s, m + jnp.log2(t), acc)
-            return acc
-
-        acc = lax.fori_loop(0, groups, group, jnp.zeros((LANES, LANES), jnp.float32))
-        lbuf[...] = acc.T[:cap]
-
-    def col_pass(pot):
+    def lse_pass(pot, ids, tiles, first):
         def collect(g, _):
             for k in range(GROUP):
                 s = g * GROUP + k
-                gbuf[pl.ds(s, 1), :] = pot[pl.ds(rows[0, 0, s], 1), :]
+                gbuf[pl.ds(s, 1), :] = pot[pl.ds(ids[0, 0, s], 1), :]
             return 0
 
         lax.fori_loop(0, groups, collect, 0)
@@ -134,18 +132,24 @@
         def group(g, _):
             base = g * GROUP
             near = pltpu.roll(turned, lax.rem(LANES - base, LANES), 1)
-            top = jnp.zeros((GROUP, LANES), jnp.float32)
-            mass = jnp.ones((GROUP, LANES), jnp.float32)
-            for k in range(GROUP):
-                x = near[:, k : k + 1] - cbuf[base + k]
-                m = jnp.max(x, axis=0, keepdims=True)
-                t = jnp.sum(jnp.exp2(x - m), axis=0, keepdims=True)
-                top = jnp.where(sub8 == k, m, top)
-                mass = jnp.where(sub8 == k, t, mass)
-            lbuf[pl.ds(pl.multiple_of(base, GROUP), GROUP), :] = top + jnp.log2(mass)
+            if first:
+                fetch(g).wait()
+                for k in range(GROUP):
+                    tile = cbuf[base + k] * SCALE
+                    cbuf[base + k] = tile
+                    tiles[base + k] = tile.T
+            for k in range(GROUP):
+                x = near[:, k : k + 1] - tiles[base + k]
+                x = x.reshape(LANES // GROUP, GROUP, LANES)
+                m = jnp.max(x, axis=0)
+                t = jnp.sum(jnp.exp2(x - m[None]), axis=0)
+                row = pl.multiple_of((base + k) * GROUP, GROUP)
+                fine[pl.ds(row, GROUP), :] = m + jnp.log2(t)
             return 0
 
         lax.fori_loop(0, groups, group, 0)
+        pieces = [fine[pl.ds(k, cap, stride=GROUP), :] for k in range(GROUP)]
+        lbuf[...] = join(pieces)
 
     def merge(ids, seg, hot, rep, part):
         mine = seg[...]
@@ -189,9 +193,7 @@
         for copy in copies:
             copy.wait_recv()
         parts += [mid[o] for o in range(n - 1)]
-        top = functools.reduce(jnp.maximum, parts)
-        total = functools.reduce(jnp.add, [jnp.exp2(p - top) for p in parts])
-        pot[own, :] = mass - (top + jnp.log2(total))
+        pot[own, :] = mass - join(parts)
         pending.extend(copies)
         copies = []
         for o in range(1, n):
@@ -213,14 +215,14 @@
     pot = init_pot
     for it in range(ITERS):
         part, mid, pot_s = source[it]
-        row_pass(pot, it == 0)
+        lse_pass(pot, cols, turned_cost, it == 0)
         merge(rows, seg_s, hot_s, rep_s, part)
         if it == 0:
             pl.semaphore_wait(barrier, n_row + n_col - 2)
         exchange("col", it, part, mid, pot_s, slog,
                  scatter_send_s, scatter_recv_s, gather_send_s, gather_recv_s)
         part, mid, pot = target[it]
-        col_pass(pot_s)
+        lse_pass(pot_s, rows, cbuf, False)
         merge(cols, seg_t, hot_t, rep_t, part)
         exchange("row", it, part, mid, pot, tlog,
                  scatter_send_t, scatter_recv_t, gather_send_t, gather_recv_t)
@@ -238,13 +240,21 @@
     nbs = source_logmass.shape[0] // width
     nbt = target_logmass.shape[0] // width
     f32, bf16 = jnp.float32, jnp.bfloat16
+    hbm = pl.BlockSpec(memory_space=pltpu.HBM)
     vmem = pl.BlockSpec(memory_space=pltpu.VMEM)
     smem = pl.BlockSpec(memory_space=pltpu.SMEM)
     dma = pltpu.SemaphoreType.DMA
     scratch = [
+        pltpu.SMEM((1, 1, cap), jnp.int32),
+        pltpu.SMEM((1, 1, cap), jnp.int32),
+        pltpu.VMEM((nbs, width), f32),
+        pltpu.VMEM((nbt, width), f32),
+        dma((5,)),
         pltpu.VMEM((cap, width, width), f32),
+        pltpu.VMEM((cap, width, width), f32),
+        pltpu.VMEM((cap * GROUP, width), f32),
         pltpu.VMEM((cap, width), f32),
-        pltpu.VMEM((cap, width), f32),
+        pltpu.VMEM((width, width), f32),
         pltpu.VMEM((nbt, width), f32),
         pltpu.VMEM((cap, width), jnp.int32),
         pltpu.VMEM((cap, width), jnp.int32),
@@ -265,11 +275,11 @@
             jax.ShapeDtypeStruct((nbs, width), f32),
             jax.ShapeDtypeStruct((nbt, width), f32),
         ),
-        in_specs=[pl.BlockSpec(memory_space=pl.ANY), smem, smem, smem, vmem, vmem, vmem],
+        in_specs=[hbm, hbm, hbm, smem, hbm, hbm, hbm],
         out_specs=(vmem, vmem),
         scratch_shapes=scratch,
         compiler_params=pltpu.CompilerParams(
-            collective_id=0, has_side_effects=True, vmem_limit_bytes=48 * 1024 * 1024
+            collective_id=0, has_side_effects=True, vmem_limit_bytes=65536 * 1024
         ),
         cost_estimate=pl.CostEstimate(
             flops=2 * ITERS * 5 * cap * width * width,

time: 59.9 us -> 53.4 us (0.89)
  local copies, waits for them, and re-layouts: 6.01 us -> 0 us
  Pallas kernels: 51.6 us -> 50.4 us
  other arithmetic: 0.66 us -> 1.53 us
    unnamed x12 -> x0, local copies, waits for them, and re-layouts: 6.01 us -> none
    pallas_call x1, Pallas kernels: 51.6 us -> 50.4 us  [local(): pl.pallas_call(functools.partial(kernel, n_row=n_row, n_col=n_col), out_s...]
    div x1, other arithmetic: 0.66 us -> 1.53 us  [local(): return (source.reshape(-1) / SCALE, target.reshape(-1) / SCALE)]
where the time goes in v2:
time: 53.4 us; the launch traced here: 53.3 us
  Pallas kernels  50.4 us (94%)
  other arithmetic  1.53 us (3%)
  between operations  1.28 us (2%)
    pallas_call x1, Pallas kernels, local(): pl.pallas_call(functools.partial(kernel, n_row=n_row, n_col=n_col), out_s...  50.4 us
    div x1, other arithmetic, local(): return (source.reshape(-1) / SCALE, target.reshape(-1) / SCALE)  1.53 us

profile of v2, /device:TPU:0, one launch (start us, length us, event | category | flops | bytes accessed | tf_op | source)
XLA Modules:
  0.0 53.3 jit_solution(8281997773838666548)
XLA Ops:
  1.3 50.4 %shard_map.86 = (f32[128,128]{1,0:T(8,128)}, f32[128,128]{1,0:T(8,128)}) custom-call(f32[1,1,64,128,128]{4,3,2,1,0:T(8,128)} %cost.1, s32[1,1,64]{2,1,0:T(1,128)} %rows_in.1, s32[1,1,64]{2,1,0:T(1,128)} %cols_in.1, s32[1,1]{1,0:T(1,128)S(6)} %copy.9.count, f32[128,128]{1,0:T(8,128)} %bitcast.7, f32[128,128]{1,0:T(8,128)} %bitcast.8, f32[128,128]{1,0:T(8,128)} %bitcast.9), custom_call_target="tpu_custom_call" | custom-call | flops 20971520 | bytes 4194304 | tf_op jit(solution)/shard_map/pallas_call | solution.py:272
  51.7 1.5 %multiply_bitcast_fusion = (f32[16384]{0:T(1024)}, f32[16384]{0:T(1024)}) fusion(f32[128,128]{1,0:T(8,128)} %get-tuple-element.5, f32[128,128]{1,0:T(8,128)} %get-tuple-element.4), kind=kLoop, calls=%fused_computation | loop fusion | flops 32768 | bytes 262144 | tf_op jit(solution)/shard_map/div | solution.py:295

commit v3 on v2

--- a/solution.py
+++ b/solution.py
@@ -13,6 +13,7 @@
 LOG2E = math.log2(math.e)
 SCALE = LOG2E / EPS
 GROUP = 8
+TILES = 16
 LANES = 128
 MESH = pl.DeviceIdType.MESH
 
@@ -36,12 +37,13 @@
     cost, rows_in, cols_in, count, slog_in, tlog_in, tinit_in,
     s_out, t_out,
     rows, cols, slog, tlog, small_sem,
-    cbuf, turned_cost, fine, lbuf, gbuf, init_pot, seg_s, seg_t, hot_s, hot_t, rep_s, rep_t,
-    part_s0, part_s1, part_t0, part_t1,
+    cbuf, turned_cost, fine, lbuf, gbuf, init_pot, seg_s, seg_t,
+    same_s, first_s, first_in, place_s, absent_s, hot_t, rep_t,
+    slots_s0, slots_s1, part_t0, part_t1,
     mid_s0, mid_s1, mid_t0, mid_t1,
     pot_s0, pot_s1, pot_t0, pot_t1,
-    cost_sem, scatter_send_s, scatter_recv_s, gather_send_s, gather_recv_s,
-    scatter_send_t, scatter_recv_t, gather_send_t, gather_recv_t,
+    cost_sem, first_send, first_recv, slots_send, slots_recv,
+    scatter_send_t, scatter_recv_t, gather_send_t, gather_recv_t, out_sem,
     *, n_row, n_col,
 ):
     cap = cbuf.shape[0]
@@ -58,10 +60,10 @@
                 barrier, inc=1, device_id={axis: peer(axis, o)}, device_id_type=MESH
             )
 
-    groups = cap // GROUP
+    groups = cap // TILES
 
     def fetch(g):
-        span = pl.ds(g * GROUP, GROUP)
+        span = pl.ds(g * TILES, TILES)
         return pltpu.make_async_copy(cost.at[0, 0, span], cbuf.at[span], cost_sem.at[g])
 
     small = [
@@ -83,9 +85,7 @@
     def segment(ids, s):
         return jnp.where(s < total, ids[0, 0, s], -1)
 
-    def prepare(ids, seg, hot, rep):
-        nb = hot.shape[0]
-
+    def prepare(ids, seg, nb):
         def fill(g, _):
             value = jnp.zeros((GROUP, LANES), jnp.int32)
             for k in range(GROUP):
@@ -93,7 +93,7 @@
             seg[pl.ds(pl.multiple_of(g * GROUP, GROUP), GROUP), :] = value
             return 0
 
-        lax.fori_loop(0, groups, fill, 0)
+        lax.fori_loop(0, cap // GROUP, fill, 0)
         mine = seg[...]
 
         def earlier(g, dup):
@@ -103,26 +103,44 @@
                 dup = jnp.where(same, 1.0, dup)
             return dup
 
-        dup = lax.fori_loop(0, groups, earlier, jnp.zeros((cap, LANES), jnp.float32))
+        dup = jnp.zeros((cap, LANES), jnp.float32)
+        dup = lax.fori_loop(0, cap // GROUP, earlier, dup)
         blocks = lax.broadcasted_iota(jnp.int32, (cap, nb), 1)
         one = jnp.where(mine[:, :nb] == blocks, 1.0, 0.0)
-        first = one * (1.0 - dup[:, :nb])
+        return one, one * (1.0 - dup[:, :nb])
+
+    def prepare_source():
+        one, first = prepare(rows, seg_s, first_s.shape[1])
+        first_s[...] = first
+        one = one.astype(jnp.bfloat16)
+        same = lax.dot_general(
+            one, one, (((1,), (1,)), ((), ())), preferred_element_type=jnp.float32
+        )
+        same_s[...] = jnp.concatenate([same, same], axis=1).astype(jnp.bfloat16)
+
+    def prepare_target():
+        one, first = prepare(cols, seg_t, hot_t.shape[0])
         both = jnp.concatenate([one, first], axis=0).T
         one, first = both[:, :cap], both[:, cap:]
-        hot[...] = jnp.concatenate([one, one], axis=1).astype(jnp.bfloat16)
-        rep[...] = jnp.concatenate([first] * 4, axis=1).astype(jnp.bfloat16)
+        hot_t[...] = jnp.concatenate([one, one], axis=1).astype(jnp.bfloat16)
+        rep_t[...] = jnp.concatenate([first] * 4, axis=1).astype(jnp.bfloat16)
+
+    def prepare_place(q, first):
+        first = first.T
+        place_s[q] = jnp.concatenate([first] * 4, axis=1).astype(jnp.bfloat16)
+        found = jnp.sum(first, axis=1, keepdims=True)
+        absent_s[q] = jnp.broadcast_to(jnp.where(found > 0.0, 0.0, -1e30), absent_s.shape[1:])
 
     gbuf[...] = jnp.zeros_like(gbuf)
     for copy in small:
         copy.wait()
     init_pot[...] = init_pot[...] * SCALE
-    prepare(rows, seg_s, hot_s, rep_s)
-    prepare(cols, seg_t, hot_t, rep_t)
+    prepare_source()
 
     def lse_pass(pot, ids, tiles, first):
         def collect(g, _):
-            for k in range(GROUP):
-                s = g * GROUP + k
+            for k in range(TILES):
+                s = g * TILES + k
                 gbuf[pl.ds(s, 1), :] = pot[pl.ds(ids[0, 0, s], 1), :]
             return 0
 
@@ -130,15 +148,15 @@
         turned = gbuf[...].T
 
         def group(g, _):
-            base = g * GROUP
+            base = g * TILES
             near = pltpu.roll(turned, lax.rem(LANES - base, LANES), 1)
             if first:
                 fetch(g).wait()
-                for k in range(GROUP):
+                for k in range(TILES):
                     tile = cbuf[base + k] * SCALE
                     cbuf[base + k] = tile
                     tiles[base + k] = tile.T
-            for k in range(GROUP):
+            for k in range(TILES):
                 x = near[:, k : k + 1] - tiles[base + k]
                 x = x.reshape(LANES // GROUP, GROUP, LANES)
                 m = jnp.max(x, axis=0)
@@ -151,7 +169,7 @@
         pieces = [fine[pl.ds(k, cap, stride=GROUP), :] for k in range(GROUP)]
         lbuf[...] = join(pieces)
 
-    def merge(ids, seg, hot, rep, part):
+    def level(ids, seg):
         mine = seg[...]
         own = lbuf[...]
 
@@ -162,15 +180,44 @@
                 best = jnp.where(mine == segment(ids, t), other, best)
             return best
 
-        best = lax.fori_loop(0, groups, widen, own)
-        weight = jnp.concatenate(split_bf16(jnp.exp2(own - best), 2), axis=0)
-        tops = split_bf16(best, 3)
-        tops = jnp.concatenate(tops + [jnp.zeros_like(tops[0])], axis=0)
-        mass = jnp.dot(hot[...], weight, preferred_element_type=jnp.float32)
-        peak = jnp.dot(rep[...], tops, preferred_element_type=jnp.float32)
+        best = lax.fori_loop(0, cap // GROUP, widen, own)
+        return best, jnp.concatenate(split_bf16(jnp.exp2(own - best), 2), axis=0)
+
+    def thirds(x):
+        parts = split_bf16(x, 3)
+        return jnp.concatenate(parts + [jnp.zeros_like(parts[0])], axis=0)
+
+    def merge_source(slots):
+        best, weight = level(rows, seg_s)
+        mass = jnp.dot(same_s[...], weight, preferred_element_type=jnp.float32)
+        slots[...] = best + jnp.log2(jnp.maximum(mass, 1.0))
+
+    def merge_target(part):
+        best, weight = level(cols, seg_t)
+        mass = jnp.dot(hot_t[...], weight, preferred_element_type=jnp.float32)
+        peak = jnp.dot(rep_t[...], thirds(best), preferred_element_type=jnp.float32)
         part[...] = jnp.where(mass > 0.0, peak + jnp.log2(mass), -1e30)
 
     pending = []
+
+    def send_all(axis, src, inbox, send, recv):
+        copies = []
+        for o in range(1, sizes[axis]):
+            copies.append(pltpu.make_async_remote_copy(
+                src_ref=src,
+                dst_ref=inbox.at[o - 1],
+                send_sem=send.at[o - 1],
+                recv_sem=recv.at[o - 1],
+                device_id={axis: peer(axis, o)},
+                device_id_type=MESH,
+            ))
+            copies[-1].start()
+        pending.extend(copies)
+        return copies
+
+    def place(q, slots):
+        spread = jnp.dot(place_s[q], thirds(slots), preferred_element_type=jnp.float32)
+        return spread + absent_s[q]
 
     def exchange(axis, it, part, mid, pot, logmass, s_send, s_recv, g_send, g_recv):
         n = sizes[axis]
@@ -210,26 +257,42 @@
             copy.wait_recv()
         pending.extend(copies)
 
-    source = ((part_s0, mid_s0, pot_s0), (part_s1, mid_s1, pot_s1))
+    pl.semaphore_wait(barrier, n_row + n_col - 2)
+    firsts = send_all("col", first_s, first_in, first_send, first_recv)
+    prepare_place(0, first_s[...])
+
+    source = ((slots_s0, mid_s0, pot_s0), (slots_s1, mid_s1, pot_s1))
     target = ((part_t0, mid_t0, pot_t0), (part_t1, mid_t1, pot_t1))
     pot = init_pot
     for it in range(ITERS):
-        part, mid, pot_s = source[it]
+        slots, inbox, pot_s = source[it]
         lse_pass(pot, cols, turned_cost, it == 0)
-        merge(rows, seg_s, hot_s, rep_s, part)
+        merge_source(slots)
+        copies = send_all("col", slots, inbox, slots_send.at[it], slots_recv.at[it])
         if it == 0:
-            pl.semaphore_wait(barrier, n_row + n_col - 2)
-        exchange("col", it, part, mid, pot_s, slog,
-                 scatter_send_s, scatter_recv_s, gather_send_s, gather_recv_s)
+            prepare_target()
+            for q, copy in enumerate(firsts):
+                copy.wait_recv()
+                prepare_place(q + 1, first_in[q])
+        parts = [place(0, slots[...])]
+        for q, copy in enumerate(copies):
+            copy.wait_recv()
+            parts.append(place(q + 1, inbox[q]))
+        pot_s[...] = slog[...] * LOG2E - join(parts)
+        if it == ITERS - 1:
+            out_copy = pltpu.make_async_copy(pot_s, s_out, out_sem.at[0])
+            out_copy.start()
         part, mid, pot = target[it]
         lse_pass(pot_s, rows, cbuf, False)
-        merge(cols, seg_t, hot_t, rep_t, part)
+        merge_target(part)
         exchange("row", it, part, mid, pot, tlog,
                  scatter_send_t, scatter_recv_t, gather_send_t, gather_recv_t)
-    s_out[...] = pot_s[...]
-    t_out[...] = pot[...]
+    last_copy = pltpu.make_async_copy(pot, t_out, out_sem.at[1])
+    last_copy.start()
     for copy in pending:
         copy.wait_send()
+    out_copy.wait()
+    last_copy.wait()
 
 
 def local(
@@ -241,7 +304,6 @@
     nbt = target_logmass.shape[0] // width
     f32, bf16 = jnp.float32, jnp.bfloat16
     hbm = pl.BlockSpec(memory_space=pltpu.HBM)
-    vmem = pl.BlockSpec(memory_space=pltpu.VMEM)
     smem = pl.BlockSpec(memory_space=pltpu.SMEM)
     dma = pltpu.SemaphoreType.DMA
     scratch = [
@@ -258,17 +320,21 @@
         pltpu.VMEM((nbt, width), f32),
         pltpu.VMEM((cap, width), jnp.int32),
         pltpu.VMEM((cap, width), jnp.int32),
-        pltpu.VMEM((nbs, 2 * cap), bf16),
+        pltpu.VMEM((cap, 2 * cap), bf16),
+        pltpu.VMEM((cap, nbs), f32),
+        pltpu.VMEM((n_col - 1, cap, nbs), f32),
+        pltpu.VMEM((n_col, nbs, 4 * cap), bf16),
+        pltpu.VMEM((n_col, nbs, width), f32),
         pltpu.VMEM((nbt, 2 * cap), bf16),
-        pltpu.VMEM((nbs, 4 * cap), bf16),
         pltpu.VMEM((nbt, 4 * cap), bf16),
     ]
-    scratch += [pltpu.VMEM((nbs, width), f32)] * 2 + [pltpu.VMEM((nbt, width), f32)] * 2
-    scratch += [pltpu.VMEM((n_col - 1, nbs // n_col, width), f32)] * 2
+    scratch += [pltpu.VMEM((cap, width), f32)] * 2 + [pltpu.VMEM((nbt, width), f32)] * 2
+    scratch += [pltpu.VMEM((n_col - 1, cap, width), f32)] * 2
     scratch += [pltpu.VMEM((n_row - 1, nbt // n_row, width), f32)] * 2
     scratch += [pltpu.VMEM((nbs, width), f32)] * 2 + [pltpu.VMEM((nbt, width), f32)] * 2
-    scratch += [dma((cap // GROUP,))]
-    scratch += [dma((ITERS, n_col - 1))] * 4 + [dma((ITERS, n_row - 1))] * 4
+    scratch += [dma((cap // TILES,))]
+    scratch += [dma((n_col - 1,))] * 2 + [dma((ITERS, n_col - 1))] * 2
+    scratch += [dma((ITERS, n_row - 1))] * 4 + [dma((2,))]
     source, target = pl.pallas_call(
         functools.partial(kernel, n_row=n_row, n_col=n_col),
         out_shape=(
@@ -276,7 +342,7 @@
             jax.ShapeDtypeStruct((nbt, width), f32),
         ),
         in_specs=[hbm, hbm, hbm, smem, hbm, hbm, hbm],
-        out_specs=(vmem, vmem),
+        out_specs=(hbm, hbm),
         scratch_shapes=scratch,
         compiler_params=pltpu.CompilerParams(
             collective_id=0, has_side_effects=True, vmem_limit_bytes=65536 * 1024

time: 53.4 us -> 44.9 us (0.84)
  Pallas kernels: 50.4 us -> 41.9 us
    pallas_call x1, Pallas kernels: 50.4 us -> 41.9 us  [local(): pl.pallas_call(functools.partial(kernel, n_row=n_row, n_col=n_col), out_s...]
where the time goes in v3:
time: 44.9 us; the launch traced here: 44.7 us
  Pallas kernels  41.9 us (93%)
  other arithmetic  1.53 us (3%)
  between operations  1.28 us (3%)
    pallas_call x1, Pallas kernels, local(): pl.pallas_call(functools.partial(kernel, n_row=n_row, n_col=n_col), out_s...  41.9 us
    div x1, other arithmetic, local(): return (source.reshape(-1) / SCALE, target.reshape(-1) / SCALE)  1.53 us

profile of v3, /device:TPU:0, one launch (start us, length us, event | category | flops | bytes accessed | tf_op | source)
XLA Modules:
  0.0 44.7 jit_solution(11374629346277971260)
XLA Ops:
  1.3 41.9 %shard_map.86 = (f32[128,128]{1,0:T(8,128)}, f32[128,128]{1,0:T(8,128)}) custom-call(f32[1,1,64,128,128]{4,3,2,1,0:T(8,128)} %cost.1, s32[1,1,64]{2,1,0:T(1,128)} %rows_in.1, s32[1,1,64]{2,1,0:T(1,128)} %cols_in.1, s32[1,1]{1,0:T(1,128)S(6)} %copy.9.count, f32[128,128]{1,0:T(8,128)} %bitcast.7, f32[128,128]{1,0:T(8,128)} %bitcast.8, f32[128,128]{1,0:T(8,128)} %bitcast.9), custom_call_target="tpu_custom_call" | custom-call | flops 20971520 | bytes 4194304 | tf_op jit(solution)/shard_map/pallas_call | solution.py:338
  43.2 1.5 %multiply_bitcast_fusion = (f32[16384]{0:T(1024)}, f32[16384]{0:T(1024)}) fusion(f32[128,128]{1,0:T(8,128)} %get-tuple-element.5, f32[128,128]{1,0:T(8,128)} %get-tuple-element.4), kind=kLoop, calls=%fused_computation | loop fusion | flops 32768 | bytes 262144 | tf_op jit(solution)/shard_map/div | solution.py:361

commit v4 on v3

--- a/solution.py
+++ b/solution.py
@@ -14,6 +14,7 @@
 SCALE = LOG2E / EPS
 GROUP = 8
 TILES = 16
+WIDE = 32
 LANES = 128
 MESH = pl.DeviceIdType.MESH
 
@@ -37,13 +38,13 @@
     cost, rows_in, cols_in, count, slog_in, tlog_in, tinit_in,
     s_out, t_out,
     rows, cols, slog, tlog, small_sem,
-    cbuf, turned_cost, fine, lbuf, gbuf, init_pot, seg_s, seg_t,
+    cbuf, turned_cost, fine, lbuf, gbuf, near, moved, init_pot, seg_s, seg_t,
     same_s, first_s, first_in, place_s, absent_s, hot_t, rep_t,
     slots_s0, slots_s1, part_t0, part_t1,
     mid_s0, mid_s1, mid_t0, mid_t1,
     pot_s0, pot_s1, pot_t0, pot_t1,
     cost_sem, first_send, first_recv, slots_send, slots_recv,
-    scatter_send_t, scatter_recv_t, gather_send_t, gather_recv_t, out_sem,
+    scatter_send_t, scatter_recv_t, gather_send_t, gather_recv_t,
     *, n_row, n_col,
 ):
     cap = cbuf.shape[0]
@@ -137,50 +138,70 @@
     init_pot[...] = init_pot[...] * SCALE
     prepare_source()
 
-    def lse_pass(pot, ids, tiles, first):
+    def gathered():
+        pieces = [fine[pl.ds(k, cap, stride=GROUP), :] for k in range(GROUP)]
+        lbuf[...] = join(pieces)
+
+    def fine_row(s):
+        return pl.ds(pl.multiple_of(s * GROUP, GROUP), GROUP)
+
+    def first_pass():
+        def group(g, _):
+            base = g * TILES
+            fetch(g).wait()
+            for k in range(TILES):
+                s = base + k
+                tile = cbuf[s] * SCALE
+                cbuf[s] = tile
+                y = (tile - init_pot[pl.ds(cols[0, 0, s], 1), :]).T
+                turned_cost[s] = y
+                y = y.reshape(LANES // GROUP, GROUP, LANES)
+                m = jnp.min(y, axis=0)
+                t = jnp.sum(jnp.exp2(m[None] - y), axis=0)
+                fine[fine_row(s), :] = jnp.log2(t) - m
+            return 0
+
+        lax.fori_loop(0, cap // TILES, group, 0)
+        gathered()
+
+    def lse_pass(pot, ids, tiles):
         def collect(g, _):
-            for k in range(TILES):
-                s = g * TILES + k
+            for k in range(GROUP):
+                s = g * GROUP + k
                 gbuf[pl.ds(s, 1), :] = pot[pl.ds(ids[0, 0, s], 1), :]
             return 0
 
-        lax.fori_loop(0, groups, collect, 0)
+        lax.fori_loop(0, cap // GROUP, collect, 0)
         turned = gbuf[...].T
+        for g in range(cap // WIDE):
+            near[g] = turned if g == 0 else pltpu.roll(turned, LANES - g * WIDE, 1)
 
         def group(g, _):
-            base = g * TILES
-            near = pltpu.roll(turned, lax.rem(LANES - base, LANES), 1)
-            if first:
-                fetch(g).wait()
-                for k in range(TILES):
-                    tile = cbuf[base + k] * SCALE
-                    cbuf[base + k] = tile
-                    tiles[base + k] = tile.T
-            for k in range(TILES):
-                x = near[:, k : k + 1] - tiles[base + k]
+            base = g * WIDE
+            side = near[g]
+            for k in range(WIDE):
+                x = side[:, k : k + 1] - tiles[base + k]
                 x = x.reshape(LANES // GROUP, GROUP, LANES)
                 m = jnp.max(x, axis=0)
                 t = jnp.sum(jnp.exp2(x - m[None]), axis=0)
-                row = pl.multiple_of((base + k) * GROUP, GROUP)
-                fine[pl.ds(row, GROUP), :] = m + jnp.log2(t)
+                fine[fine_row(base + k), :] = m + jnp.log2(t)
             return 0
 
-        lax.fori_loop(0, groups, group, 0)
-        pieces = [fine[pl.ds(k, cap, stride=GROUP), :] for k in range(GROUP)]
-        lbuf[...] = join(pieces)
+        lax.fori_loop(0, cap // WIDE, group, 0)
+        gathered()
 
     def level(ids, seg):
         mine = seg[...]
         own = lbuf[...]
 
         def widen(g, best):
-            for k in range(GROUP):
-                t = g * GROUP + k
+            for k in range(TILES):
+                t = g * TILES + k
                 other = jnp.maximum(best, lbuf[pl.ds(t, 1), :])
                 best = jnp.where(mine == segment(ids, t), other, best)
             return best
 
-        best = lax.fori_loop(0, cap // GROUP, widen, own)
+        best = lax.fori_loop(0, cap // TILES, widen, own)
         return best, jnp.concatenate(split_bf16(jnp.exp2(own - best), 2), axis=0)
 
     def thirds(x):
@@ -266,7 +287,11 @@
     pot = init_pot
     for it in range(ITERS):
         slots, inbox, pot_s = source[it]
-        lse_pass(pot, cols, turned_cost, it == 0)
+        if it == 0:
+            first_pass()
+        else:
+            moved[...] = pot[...] - init_pot[...]
+            lse_pass(moved, cols, turned_cost)
         merge_source(slots)
         copies = send_all("col", slots, inbox, slots_send.at[it], slots_recv.at[it])
         if it == 0:
@@ -280,19 +305,15 @@
             parts.append(place(q + 1, inbox[q]))
         pot_s[...] = slog[...] * LOG2E - join(parts)
         if it == ITERS - 1:
-            out_copy = pltpu.make_async_copy(pot_s, s_out, out_sem.at[0])
-            out_copy.start()
+            s_out[...] = pot_s[...]
         part, mid, pot = target[it]
-        lse_pass(pot_s, rows, cbuf, False)
+        lse_pass(pot_s, rows, cbuf)
         merge_target(part)
         exchange("row", it, part, mid, pot, tlog,
                  scatter_send_t, scatter_recv_t, gather_send_t, gather_recv_t)
-    last_copy = pltpu.make_async_copy(pot, t_out, out_sem.at[1])
-    last_copy.start()
+    t_out[...] = pot[...]
     for copy in pending:
         copy.wait_send()
-    out_copy.wait()
-    last_copy.wait()
 
 
 def local(
@@ -303,6 +324,7 @@
     nbs = source_logmass.shape[0] // width
     nbt = target_logmass.shape[0] // width
     f32, bf16 = jnp.float32, jnp.bfloat16
+    vmem = pl.BlockSpec(memory_space=pltpu.VMEM)
     hbm = pl.BlockSpec(memory_space=pltpu.HBM)
     smem = pl.BlockSpec(memory_space=pltpu.SMEM)
     dma = pltpu.SemaphoreType.DMA
@@ -317,6 +339,8 @@
         pltpu.VMEM((cap * GROUP, width), f32),
         pltpu.VMEM((cap, width), f32),
         pltpu.VMEM((width, width), f32),
+        pltpu.VMEM((cap // WIDE, width, width), f32),
+        pltpu.VMEM((nbt, width), f32),
         pltpu.VMEM((nbt, width), f32),
         pltpu.VMEM((cap, width), jnp.int32),
         pltpu.VMEM((cap, width), jnp.int32),
@@ -334,18 +358,18 @@
     scratch += [pltpu.VMEM((nbs, width), f32)] * 2 + [pltpu.VMEM((nbt, width), f32)] * 2
     scratch += [dma((cap // TILES,))]
     scratch += [dma((n_col - 1,))] * 2 + [dma((ITERS, n_col - 1))] * 2
-    scratch += [dma((ITERS, n_row - 1))] * 4 + [dma((2,))]
+    scratch += [dma((ITERS, n_row - 1))] * 4
     source, target = pl.pallas_call(
         functools.partial(kernel, n_row=n_row, n_col=n_col),
         out_shape=(
-            jax.ShapeDtypeStruct((nbs, width), f32),
-            jax.ShapeDtypeStruct((nbt, width), f32),
+            pltpu.VMEM((nbs, width), f32),
+            pltpu.VMEM((nbt, width), f32),
         ),
         in_specs=[hbm, hbm, hbm, smem, hbm, hbm, hbm],
-        out_specs=(hbm, hbm),
+        out_specs=(vmem, vmem),
         scratch_shapes=scratch,
         compiler_params=pltpu.CompilerParams(
-            collective_id=0, has_side_effects=True, vmem_limit_bytes=65536 * 1024
+            collective_id=0, has_side_effects=True, vmem_limit_bytes=64512 * 1024
         ),
         cost_estimate=pl.CostEstimate(
             flops=2 * ITERS * 5 * cap * width * width,

time: 44.9 us -> 40.4 us (0.90)
  Pallas kernels: 41.9 us -> 38.3 us
  other arithmetic: 1.53 us -> 0.66 us
    pallas_call x1, Pallas kernels: 41.9 us -> 38.3 us  [local(): pl.pallas_call(functools.partial(kernel, n_row=n_row, n_col=n_col), out_s...]
    div x1, other arithmetic: 1.53 us -> 0.66 us  [local(): return (source.reshape(-1) / SCALE, target.reshape(-1) / SCALE)]
where the time goes in v4:
time: 40.4 us; the launch traced here: 40.2 us
  Pallas kernels  38.3 us (95%)
  between operations  1.28 us (3%)
  other arithmetic  0.66 us (2%)
    pallas_call x1, Pallas kernels, local(): pl.pallas_call(functools.partial(kernel, n_row=n_row, n_col=n_col), out_s...  38.3 us

profile of v4, /device:TPU:0, one launch (start us, length us, event | category | flops | bytes accessed | tf_op | source)
XLA Modules:
  0.0 40.2 jit_solution(10728634497925983108)
XLA Ops:
  1.3 38.3 %shard_map.86 = (f32[128,128]{1,0:T(8,128)S(1)}, f32[128,128]{1,0:T(8,128)S(1)}) custom-call(f32[1,1,64,128,128]{4,3,2,1,0:T(8,128)} %cost.1, s32[1,1,64]{2,1,0:T(1,128)} %rows_in.1, s32[1,1,64]{2,1,0:T(1,128)} %cols_in.1, s32[1,1]{1,0:T(1,128)S(6)} %copy.9.count, f32[128,128]{1,0:T(8,128)} %bitcast.7, f32[128,128]{1,0:T(8,128)} %bitcast.8, f32[128,128]{1,0:T(8,128)} %bitcast.9), custom_call_target="tpu_custom_call" | custom-call | flops 20971520 | bytes 4194304 | tf_op jit(solution)/shard_map/pallas_call | solution.py:362
  39.5 0.7 %multiply_bitcast_fusion = (f32[16384]{0:T(1024)}, f32[16384]{0:T(1024)}) fusion(f32[128,128]{1,0:T(8,128)S(1)} %get-tuple-element.5, f32[128,128]{1,0:T(8,128)S(1)} %get-tuple-element.4), kind=kLoop, calls=%fused_computation | loop fusion | flops 32768 | bytes 262144 | tf_op jit(solution)/shard_map/div | solution.py:385

commit v5 on v4

--- a/solution.py
+++ b/solution.py
@@ -38,7 +38,7 @@
     cost, rows_in, cols_in, count, slog_in, tlog_in, tinit_in,
     s_out, t_out,
     rows, cols, slog, tlog, small_sem,
-    cbuf, turned_cost, fine, lbuf, gbuf, near, moved, init_pot, seg_s, seg_t,
+    cbuf, turned_cost, fine, lbuf, gbuf, moved, init_pot, seg_s, seg_t,
     same_s, first_s, first_in, place_s, absent_s, hot_t, rep_t,
     slots_s0, slots_s1, part_t0, part_t1,
     mid_s0, mid_s1, mid_t0, mid_t1,
@@ -147,10 +147,11 @@
 
     def first_pass():
         def group(g, _):
-            base = g * TILES
-            fetch(g).wait()
-            for k in range(TILES):
+            base = g * WIDE
+            for k in range(WIDE):
                 s = base + k
+                if k % TILES == 0:
+                    fetch(g * (WIDE // TILES) + k // TILES).wait()
                 tile = cbuf[s] * SCALE
                 cbuf[s] = tile
                 y = (tile - init_pot[pl.ds(cols[0, 0, s], 1), :]).T
@@ -161,33 +162,19 @@
                 fine[fine_row(s), :] = jnp.log2(t) - m
             return 0
 
-        lax.fori_loop(0, cap // TILES, group, 0)
+        lax.fori_loop(0, cap // WIDE, group, 0)
         gathered()
 
     def lse_pass(pot, ids, tiles):
-        def collect(g, _):
-            for k in range(GROUP):
-                s = g * GROUP + k
-                gbuf[pl.ds(s, 1), :] = pot[pl.ds(ids[0, 0, s], 1), :]
-            return 0
-
-        lax.fori_loop(0, cap // GROUP, collect, 0)
-        turned = gbuf[...].T
-        for g in range(cap // WIDE):
-            near[g] = turned if g == 0 else pltpu.roll(turned, LANES - g * WIDE, 1)
-
-        def group(g, _):
-            base = g * WIDE
-            side = near[g]
-            for k in range(WIDE):
-                x = side[:, k : k + 1] - tiles[base + k]
-                x = x.reshape(LANES // GROUP, GROUP, LANES)
-                m = jnp.max(x, axis=0)
-                t = jnp.sum(jnp.exp2(x - m[None]), axis=0)
-                fine[fine_row(base + k), :] = m + jnp.log2(t)
-            return 0
-
-        lax.fori_loop(0, cap // WIDE, group, 0)
+        for s in range(cap):
+            gbuf[s : s + 1, :] = pot[pl.ds(ids[0, 0, s], 1), :]
+        side = gbuf[...].T
+        for s in range(cap):
+            x = side[:, s : s + 1] - tiles[s]
+            x = x.reshape(LANES // GROUP, GROUP, LANES)
+            m = jnp.max(x, axis=0)
+            t = jnp.sum(jnp.exp2(x - m[None]), axis=0)
+            fine[s * GROUP : (s + 1) * GROUP, :] = m + jnp.log2(t)
         gathered()
 
     def level(ids, seg):
@@ -195,13 +182,13 @@
         own = lbuf[...]
 
         def widen(g, best):
-            for k in range(TILES):
-                t = g * TILES + k
+            for k in range(WIDE):
+                t = g * WIDE + k
                 other = jnp.maximum(best, lbuf[pl.ds(t, 1), :])
                 best = jnp.where(mine == segment(ids, t), other, best)
             return best
 
-        best = lax.fori_loop(0, cap // TILES, widen, own)
+        best = lax.fori_loop(0, cap // WIDE, widen, own)
         return best, jnp.concatenate(split_bf16(jnp.exp2(own - best), 2), axis=0)
 
     def thirds(x):
@@ -339,7 +326,6 @@
         pltpu.VMEM((cap * GROUP, width), f32),
         pltpu.VMEM((cap, width), f32),
         pltpu.VMEM((width, width), f32),
-        pltpu.VMEM((cap // WIDE, width, width), f32),
         pltpu.VMEM((nbt, width), f32),
         pltpu.VMEM((nbt, width), f32),
         pltpu.VMEM((cap, width), jnp.int32),

time: 40.4 us -> 39.7 us (0.983)
  Pallas kernels: 38.3 us -> 37.6 us
    pallas_call x1, Pallas kernels: 38.3 us -> 37.6 us  [local(): pl.pallas_call(functools.partial(kernel, n_row=n_row, n_col=n_col), out_s...]
where the time goes in v5:
time: 39.7 us; the launch traced here: 39.6 us
  Pallas kernels  37.6 us (95%)
  between operations  1.28 us (3%)
  other arithmetic  0.66 us (2%)
    pallas_call x1, Pallas kernels, local(): pl.pallas_call(functools.partial(kernel, n_row=n_row, n_col=n_col), out_s...  37.6 us

profile of v5, /device:TPU:0, one launch (start us, length us, event | category | flops | bytes accessed | tf_op | source)
XLA Modules:
  0.0 39.6 jit_solution(8812249338479319244)
XLA Ops:
  1.3 37.6 %shard_map.86 = (f32[128,128]{1,0:T(8,128)S(1)}, f32[128,128]{1,0:T(8,128)S(1)}) custom-call(f32[1,1,64,128,128]{4,3,2,1,0:T(8,128)} %cost.1, s32[1,1,64]{2,1,0:T(1,128)} %rows_in.1, s32[1,1,64]{2,1,0:T(1,128)} %cols_in.1, s32[1,1]{1,0:T(1,128)S(6)} %copy.9.count, f32[128,128]{1,0:T(8,128)} %bitcast.7, f32[128,128]{1,0:T(8,128)} %bitcast.8, f32[128,128]{1,0:T(8,128)} %bitcast.9), custom_call_target="tpu_custom_call" | custom-call | flops 20971520 | bytes 4194304 | tf_op jit(solution)/shard_map/pallas_call | solution.py:348
  38.9 0.7 %multiply_bitcast_fusion = (f32[16384]{0:T(1024)}, f32[16384]{0:T(1024)}) fusion(f32[128,128]{1,0:T(8,128)S(1)} %get-tuple-element.5, f32[128,128]{1,0:T(8,128)S(1)} %get-tuple-element.4), kind=kLoop, calls=%fused_computation | loop fusion | flops 32768 | bytes 262144 | tf_op jit(solution)/shard_map/div | solution.py:371

commit v6 on v5

--- a/solution.py
+++ b/solution.py
@@ -79,9 +79,7 @@
         fetch(g).start()
 
     total = count[0, 0]
-    lane = lax.broadcasted_iota(jnp.int32, (LANES, LANES), 1)
     sub8 = lax.broadcasted_iota(jnp.int32, (GROUP, LANES), 0)
-    slot = lax.broadcasted_iota(jnp.int32, (cap, LANES), 0)
 
     def segment(ids, s):
         return jnp.where(s < total, ids[0, 0, s], -1)
@@ -97,30 +95,24 @@
         lax.fori_loop(0, cap // GROUP, fill, 0)
         mine = seg[...]
 
-        def earlier(g, dup):
-            for k in range(GROUP):
-                t = g * GROUP + k
-                same = (mine == segment(ids, t)) & (slot > t)
-                dup = jnp.where(same, 1.0, dup)
-            return dup
-
-        dup = jnp.zeros((cap, LANES), jnp.float32)
-        dup = lax.fori_loop(0, cap // GROUP, earlier, dup)
         blocks = lax.broadcasted_iota(jnp.int32, (cap, nb), 1)
         one = jnp.where(mine[:, :nb] == blocks, 1.0, 0.0)
-        return one, one * (1.0 - dup[:, :nb])
+        half = one.astype(jnp.bfloat16)
+        same = lax.dot_general(
+            half, half, (((1,), (1,)), ((), ())), preferred_element_type=jnp.float32
+        )
+        across = lax.broadcasted_iota(jnp.int32, (cap, cap), 1)
+        down = lax.broadcasted_iota(jnp.int32, (cap, cap), 0)
+        before = jnp.sum(jnp.where(across < down, same, 0.0), axis=1, keepdims=True)
+        return one, jnp.where(before > 0.0, 0.0, one), same
 
     def prepare_source():
-        one, first = prepare(rows, seg_s, first_s.shape[1])
+        _, first, same = prepare(rows, seg_s, first_s.shape[1])
         first_s[...] = first
-        one = one.astype(jnp.bfloat16)
-        same = lax.dot_general(
-            one, one, (((1,), (1,)), ((), ())), preferred_element_type=jnp.float32
-        )
         same_s[...] = jnp.concatenate([same, same], axis=1).astype(jnp.bfloat16)
 
     def prepare_target():
-        one, first = prepare(cols, seg_t, hot_t.shape[0])
+        one, first, _ = prepare(cols, seg_t, hot_t.shape[0])
         both = jnp.concatenate([one, first], axis=0).T
         one, first = both[:, :cap], both[:, cap:]
         hot_t[...] = jnp.concatenate([one, one], axis=1).astype(jnp.bfloat16)

time: 39.7 us -> 39.7 us (level)
  no operation moved by 1% of the time
where the time goes in v6:
time: 39.7 us; the launch traced here: 39.6 us
  Pallas kernels  37.6 us (95%)
  between operations  1.28 us (3%)
  other arithmetic  0.66 us (2%)
    pallas_call x1, Pallas kernels, local(): pl.pallas_call(functools.partial(kernel, n_row=n_row, n_col=n_col), out_s...  37.6 us

profile of v6, /device:TPU:0, one launch (start us, length us, event | category | flops | bytes accessed | tf_op | source)
XLA Modules:
  0.0 39.6 jit_solution(1502434563144486967)
XLA Ops:
  1.3 37.6 %shard_map.86 = (f32[128,128]{1,0:T(8,128)S(1)}, f32[128,128]{1,0:T(8,128)S(1)}) custom-call(f32[1,1,64,128,128]{4,3,2,1,0:T(8,128)} %cost.1, s32[1,1,64]{2,1,0:T(1,128)} %rows_in.1, s32[1,1,64]{2,1,0:T(1,128)} %cols_in.1, s32[1,1]{1,0:T(1,128)S(6)} %copy.9.count, f32[128,128]{1,0:T(8,128)} %bitcast.7, f32[128,128]{1,0:T(8,128)} %bitcast.8, f32[128,128]{1,0:T(8,128)} %bitcast.9), custom_call_target="tpu_custom_call" | custom-call | flops 20971520 | bytes 4194304 | tf_op jit(solution)/shard_map/pallas_call | solution.py:340
  38.9 0.7 %multiply_bitcast_fusion = (f32[16384]{0:T(1024)}, f32[16384]{0:T(1024)}) fusion(f32[128,128]{1,0:T(8,128)S(1)} %get-tuple-element.5, f32[128,128]{1,0:T(8,128)S(1)} %get-tuple-element.4), kind=kLoop, calls=%fused_computation | loop fusion | flops 32768 | bytes 262144 | tf_op jit(solution)/shard_map/div | solution.py:363
